TPU v7x, 512 devices: a whole 4x4x16 slice. The times are simulated.
512 devices in a mesh: gx: 16 (over z), gy: 8 (over y, core), gz: 4 (over x).
Axes of the slice: x: 4, y: 4, z: 16, core: 2. Of those that a mesh axis runs over, the one named last changes fastest.
Arguments:
- prior_thermal_state: float32 [128, 128, 512], P('gx', 'gy', 'gz'), may hold values from -6 to 6
- diffusivity_root_factor: float32 [128, 128, 512], P('gx', 'gy', 'gz'), may hold values from 0.5 to 1.5
- bead_strip_energy: float32 [32768, 512], P(('gx', 'gy'), 'gz'), may hold values from -6 to 6
- holding_tile_ordinal: int32 [32768, 1], P(('gx', 'gy')), may hold values from 0 to 127; in each aligned block of 256 rows (0 to 255, 256 to 511, ...) at most 4 rows name the same one
- bead_strip_destination: int32 [32768], P(('gx', 'gy')), may hold values from 0 to 127
Outputs:
- new_temperature: float32 [128, 128, 512], P('gx', 'gy', 'gz')
- residual: float32 [128, 128, 512], P('gx', 'gy', 'gz')
- deposited: float32 [128, 128, 512], P('gx', 'gy', 'gz')
Inputs may be any that keep to these rules, and one draw needn't show every extreme that they name: `holding_tile_ordinal`: in the rows of one gx+gy position no owner is named by more than 4 rows, a bound that some block reaches.
All inputs are finite; a program needn't handle non-finite values.
Results may differ from a plain program's by a relative error of at most 0.0003.
Values sent between devices are 32-bit elements; how exact they have to be, the bound alone decides.
A program may use at most 64 MiB of HBM per device.

v0:
```python
import jax
import jax.numpy as jnp
from jax import lax
from jax.sharding import PartitionSpec as P

ITERS = 3


def extended(cells, sides, width):
    for axis, dim in sides:
        count = lax.axis_size(axis)
        ends = count - 1
        head = lax.slice_in_dim(cells, 0, width, axis=dim)
        tail = lax.slice_in_dim(cells, cells.shape[dim] - width, cells.shape[dim], axis=dim)
        cells = jnp.concatenate(
            [
                lax.ppermute(tail, axis, [(i, (i + 1) % count) for i in range(ends)]),
                cells,
                lax.ppermute(head, axis, [((i + 1) % count, i) for i in range(ends)]),
            ],
            axis=dim,
        )
    return cells


def neighbours(padded, array_extent):
    total = jnp.zeros(array_extent, jnp.float32)
    for dx in (-1, 0, 1):
        for dy in (-1, 0, 1):
            for dz in (-1, 0, 1):
                reach = abs(dx) + abs(dy) + abs(dz)
                if reach == 0:
                    continue
                weight = 0.5 ** (reach - 1)
                total = (
                    total
                    + weight
                    * padded[
                        1 + dx : 1 + dx + array_extent[0],
                        1 + dy : 1 + dy + array_extent[1],
                        1 + dz : 1 + dz + array_extent[2],
                    ]
                )
    return total


def operate(field, diffusivity_root_factor):
    padded = extended(diffusivity_root_factor * field, (("gx", 0), ("gy", 1), ("gz", 2)), 1)
    return (
        1.0 + 10.5 * diffusivity_root_factor
    ) * field - 0.5 * diffusivity_root_factor * neighbours(padded, field.shape)


def rz_sum(resid, precond):
    return lax.psum(jnp.sum(resid * precond), ("gx", "gy", "gz"))


def local(
    prior_thermal_state,
    diffusivity_root_factor,
    bead_strip_energy,
    holding_tile_ordinal,
    bead_strip_destination,
):
    size_x = lax.axis_size("gx")
    size_y = lax.axis_size("gy")
    owners = size_x * size_y
    local_first_span, local_second_span, local_third_span = prior_thermal_state.shape
    records = bead_strip_energy.shape[0]
    capacity = max(2, 2 * records // owners)
    owner = holding_tile_ordinal[:, 0]
    onehot = (owner[:, None] == jnp.arange(owners, dtype=jnp.int32)[None, :]).astype(jnp.int32)
    rank = jnp.sum(jnp.cumsum(onehot, axis=0) * onehot, axis=1) - 1
    position = owner * capacity + rank
    send_heat = (
        jnp.zeros((owners * capacity, local_third_span), jnp.float32)
        .at[position]
        .set(bead_strip_energy)
    )
    send_slot = (
        jnp.full((owners * capacity,), float(local_first_span * local_second_span), jnp.float32)
        .at[position]
        .set(bead_strip_destination.astype(jnp.float32))
    )
    got_heat, got_slot = (
        lax.all_to_all(
            send_heat.reshape(owners, capacity, local_third_span),
            ("gx", "gy"),
            split_axis=0,
            concat_axis=0,
            tiled=True,
        ),
        lax.all_to_all(
            send_slot.reshape(owners, capacity),
            ("gx", "gy"),
            split_axis=0,
            concat_axis=0,
            tiled=True,
        ),
    )
    slots = got_slot.reshape(-1).astype(jnp.int32)
    energy_received = (
        prior_thermal_state.reshape(local_first_span * local_second_span, local_third_span)
        .at[slots]
        .add(got_heat.reshape(-1, local_third_span), mode="drop")
        .reshape(local_first_span, local_second_span, local_third_span)
    )
    diag = 1.0 + 10.5 * diffusivity_root_factor
    solution = energy_received
    resid = energy_received - operate(solution, diffusivity_root_factor)
    precond = resid / diag
    direction = precond
    rz_now = rz_sum(resid, precond)
    for step in range(ITERS):
        image = operate(direction, diffusivity_root_factor)
        alpha = rz_now / lax.psum(jnp.sum(direction * image), ("gx", "gy", "gz"))
        solution = solution + alpha * direction
        resid = resid - alpha * image
        precond = resid / diag
        rz_next = rz_sum(resid, precond)
        direction = precond + rz_next / rz_now * direction
        rz_now = rz_next
    return (solution, resid, energy_received)


def solution(mesh):
    placed = (
        P("gx", "gy", "gz"),
        P("gx", "gy", "gz"),
        P(("gx", "gy"), "gz"),
        P(("gx", "gy"), None),
        P(("gx", "gy")),
    )
    return jax.shard_map(
        local,
        mesh=mesh,
        in_specs=placed,
        out_specs=(P("gx", "gy", "gz"), P("gx", "gy", "gz"), P("gx", "gy", "gz")),
        check_vma=False,
    )
```

profile of v0, /device:TPU:1, one launch (start us, length us, event | category | flops | bytes accessed | tf_op | source)
XLA Modules:
  0.0 687.7 jit_solution(17011434298065120954)
XLA Ops:
  4.8 20.6 %all-to-all-start = ((f32[128,1,4]{2,1,0:T(1,128)}), f32[128,1,4]{2,1,0:T(1,128)S(1)}, u32[]{:S(2)}, u32[]{:S(2)}) async-start(f32[128,1,4]{2,1,0:T(1,128)} %bitcast.8), calls=%async_computation | async-start | bytes 131072 | tf_op jit(solution)/shard_map/all_to_all | solution.py:93
  27.5 12.6 %all-to-all-done = f32[128,1,4]{2,1,0:T(1,128)S(1)} async-done(((f32[128,1,4]{2,1,0:T(1,128)}), f32[128,1,4]{2,1,0:T(1,128)S(1)}, u32[]{:S(2)}, u32[]{:S(2)}) %all-to-all-start) | async-done | bytes 2080 | tf_op jit(solution)/shard_map/all_to_all | solution.py:93
  40.1 5.7 all-to-all-start.1
  46.1 20.3 %all-to-all-done.1 = f32[128,4,128]{2,1,0:T(4,128)S(1)} async-done(((f32[128,4,128]{2,1,0:T(4,128)}), f32[128,4,128]{2,1,0:T(4,128)S(1)}, u32[]{:S(2)}, u32[]{:S(2)}) %all-to-all-start.1) | async-done | bytes 262176 | tf_op jit(solution)/shard_map/all_to_all | solution.py:86
  66.4 3.3 scatter_fusion
  69.8 5.3 collective-permute-start
  76.4 3.1 collective-permute-done.1
  79.5 3.6 collective-permute-start.2
  88.2 3.1 collective-permute-start.4
  93.2 4.0 collective-permute-done.5
  104.3 5.7 collective-permute-start.8
  115.1 3.1 collective-permute-start.10
  120.0 4.0 collective-permute-done.11
  125.1 100.6 %all-reduce = (f32[]{:T(128)}, f32[]{:T(128)}) all-reduce(f32[]{:T(128)} %get-tuple-element.4, f32[]{:T(128)} %get-tuple-element.3), channel_id=1, replica_groups=mesh['gx'=16,'gy'=8,'gz'=4] {'gx','gy','gz'}, use_global_device_ids=true, to_apply=%region_7.8 | all-reduce | flops 2 | bytes 16 | tf_op jit(solution)/shard_map/psum | solution.py:55
  227.6 99.1 %psum.44 = f32[]{:T(128)} all-reduce(f32[]{:T(128)} %get-tuple-element.17), channel_id=1, replica_groups=mesh['gx'=16,'gy'=8,'gz'=4] {'gx','gy','gz'}, use_global_device_ids=true, to_apply=%region_11.12 | all-reduce | flops 1 | bytes 8 | tf_op jit(solution)/shard_map/psum | solution.py:55
  328.1 3.6 collective-permute-start.12
  336.1 4.8 collective-permute-start.14
  349.1 4.1 collective-permute-done.17
  354.3 101.6 %psum.45 = f32[]{:T(128)} all-reduce(f32[]{:T(128)} %get-tuple-element.13), channel_id=1, replica_groups=mesh['gx'=16,'gy'=8,'gz'=4] {'gx','gy','gz'}, use_global_device_ids=true, to_apply=%region_13.14 | all-reduce | flops 1 | bytes 8 | tf_op jit(solution)/shard_map/psum | solution.py:116
  457.9 98.6 %psum.46 = f32[]{:T(128)} all-reduce(f32[]{:T(128)} %get-tuple-element.11), channel_id=1, replica_groups=mesh['gx'=16,'gy'=8,'gz'=4] {'gx','gy','gz'}, use_global_device_ids=true, to_apply=%region_15.16 | all-reduce | flops 1 | bytes 8 | tf_op jit(solution)/shard_map/psum | solution.py:55
  557.8 3.7 collective-permute-start.18
  565.9 4.5 collective-permute-start.20
  578.6 4.1 collective-permute-done.23
  583.8 101.9 %psum.47 = f32[]{:T(128)} all-reduce(f32[]{:T(128)} %get-tuple-element.7), channel_id=1, replica_groups=mesh['gx'=16,'gy'=8,'gz'=4] {'gx','gy','gz'}, use_global_device_ids=true, to_apply=%region_17.18 | all-reduce | flops 1 | bytes 8 | tf_op jit(solution)/shard_map/psum | solution.py:116
  (96 shorter events, 58.9 us)
Async XLA Ops:
  4.8 35.4 %all-to-all-start = ((f32[128,1,4]{2,1,0:T(1,128)}), f32[128,1,4]{2,1,0:T(1,128)S(1)}, u32[]{:S(2)}, u32[]{:S(2)}) async-start(f32[128,1,4]{2,1,0:T(1,128)} %bitcast.8), calls=%async_computation | async-start | bytes 131072 | tf_op jit(solution)/shard_map/all_to_all | solution.py:93
  40.1 26.3 %all-to-all-start.1 = ((f32[128,4,128]{2,1,0:T(4,128)}), f32[128,4,128]{2,1,0:T(4,128)S(1)}, u32[]{:S(2)}, u32[]{:S(2)}) async-start(f32[128,4,128]{2,1,0:T(4,128)} %bitcast.10), calls=%async_computation.1 | async-start | bytes 524288 | tf_op jit(solution)/shard_map/all_to_all | solution.py:86
  69.8 6.6 collective-permute-start
  75.1 4.4 collective-permute-start.1
  79.5 5.6 collective-permute-start.2
  83.2 4.9 collective-permute-start.3
  88.2 5.0 collective-permute-start.4
  91.4 5.8 collective-permute-start.5
  97.7 3.6 collective-permute-start.6
  99.9 4.4 collective-permute-start.7
  104.3 7.6 %collective-permute-start.8 = (f32[10,1,128]{2,1,0:T(1,128)S(1)}, f32[10,1,128]{2,1,0:T(1,128)S(1)}, u32[]{:S(2)}, u32[]{:S(2)}) collective-permute-start(f32[10,1,128]{2,1,0:T(1,128)S(1)} %get-tuple-element.48), channel_id=1, source_target_pairs={{0,4},{4,8},{8,12},{12,16},{16,20},{20,24},{24,28},{1,5},{5,9},{9,... | collective-permute-start | bytes 15368 | tf_op jit(solution)/shard_map/ppermute | solution.py:17
  110.0 4.9 collective-permute-start.9
  115.1 5.0 collective-permute-start.10
  118.2 5.8 collective-permute-start.11
  328.1 4.9 collective-permute-start.12
  331.7 4.4 collective-permute-start.13
  336.1 6.7 collective-permute-start.14
  340.9 4.9 collective-permute-start.15
  347.3 6.0 collective-permute-start.17
  557.8 5.0 collective-permute-start.18
  561.5 4.4 collective-permute-start.19
  565.9 6.4 collective-permute-start.20
  570.4 4.9 collective-permute-start.21
  576.8 5.9 collective-permute-start.23
  (7 other events, 648.7 us)
where the time goes:
time: 689 us; the launch traced here: 688 us
  blocking collectives  502 us (73%)
  starting transfers between devices  86.5 us (13%)
  waiting for transfers between devices  75.5 us (11%)
  other arithmetic  9.74 us (1%)
  between operations  7.9 us (1%)
    psum x3, blocking collectives, rz_sum(): return lax.psum(jnp.sum(resid * precond), ('gx', 'gy', 'gz'))  298 us
    psum x2, blocking collectives, local(): alpha = rz_now / lax.psum(jnp.sum(direction * image), ('gx', 'gy', 'gz'))  204 us
    ppermute x12, starting transfers between devices, extended(): lax.ppermute(tail, axis, [(i, (i + 1) % count) for i in range(ends)])  42.2 us
    ppermute x12, waiting for transfers between devices, extended(): lax.ppermute(head, axis, [((i + 1) % count, i) for i in range(ends)])  40.5 us
    all_to_all x1, starting transfers between devices, local(): lax.all_to_all(send_slot.reshape(owners, capacity), ('gx', 'gy'), split_a...  20.6 us
    all_to_all x1, waiting for transfers between devices, local(): lax.all_to_all(send_heat.reshape(owners, capacity, local_third_span), ('g...  20.3 us
    ppermute x12, starting transfers between devices, extended(): lax.ppermute(head, axis, [((i + 1) % count, i) for i in range(ends)])  18 us
  transfers between devices with their start and end apart: 26, of which 18 were waited for; matrix products, arithmetic and copies ran while one was open for 0% of the time, Pallas kernels for 0%

commit v1 on v0

v1 whole, which is shorter than its diff:
```python
import functools

import jax
import jax.numpy as jnp
from jax import lax
from jax.experimental import pallas as pl
from jax.experimental.pallas import tpu as pltpu
from jax.sharding import PartitionSpec as P

MESH = pl.DeviceIdType.MESH
F32 = jnp.float32
BF16 = jnp.bfloat16
NX, NY, NZ = 16, 8, 4
CX, CY, CZ = 8, 16, 128
EX, EY = 16, 24
CAP = 4
AROUND = [(a, b, c) for a in (-1, 0, 1) for b in (-1, 0, 1) for c in (-1, 0, 1) if (a, b, c) != (0, 0, 0)]


def iota(shape, dim):
    return lax.broadcasted_iota(jnp.int32, shape, dim)


def dot_nn(a, b):
    return lax.dot_general(a, b, (((1,), (0,)), ((), ())), preferred_element_type=F32)


def dot_nt(a, b):
    return lax.dot_general(a, b, (((1,), (1,)), ((), ())), preferred_element_type=F32)


def three(v):
    hi = v.astype(BF16)
    rest = v - hi.astype(F32)
    mid = rest.astype(BF16)
    low = (rest - mid.astype(F32)).astype(BF16)
    return jnp.concatenate([hi, mid, low], axis=1)


def picked(onehot, parts):
    out = dot_nn(onehot, parts)
    n = out.shape[1] // 3
    return (out[:, 2 * n :] + out[:, n : 2 * n]) + out[:, :n]


def two_sum(a, b):
    s = a + b
    t = s - a
    return s, (a - (s - t)) + (b - t)


def quick_sum(a, b):
    s = a + b
    return s, b - (s - a)


def halves(a):
    c = a * 4097.0
    hi = c - (c - a)
    return hi, a - hi


def two_prod(a, b, sa=None, sb=None):
    p = a * b
    ah, al = halves(a) if sa is None else sa
    bh, bl = halves(b) if sb is None else sb
    return p, ((ah * bh - p) + ah * bl + al * bh) + al * bl


def dd_add(a, b):
    s, e = two_sum(a[0], b[0])
    return quick_sum(s, e + (a[1] + b[1]))


def dd_neg(a):
    return -a[0], -a[1]


def dd_sub(a, b):
    return dd_add(a, dd_neg(b))


def dd_mul(a, b):
    p, e = two_prod(a[0], b[0])
    return quick_sum(p, e + (a[0] * b[1] + a[1] * b[0]))


def dd_div(a, b):
    q = a[0] / b[0]
    r = dd_sub(a, dd_mul((q, jnp.zeros_like(q)), b))
    q2 = r[0] / b[0]
    r = dd_sub(r, dd_mul((q2, jnp.zeros_like(q)), b))
    return dd_add(quick_sum(q, q2), (r[0] / b[0], jnp.zeros_like(q)))


def tree(values, add):
    while len(values) > 1:
        values = [add(*values[i : i + 2]) if i + 1 < len(values) else values[i] for i in range(0, len(values), 2)]
    return values[0]


def coefficients(m):
    d = [dd_sub(m[k], m[k + 1]) for k in range(5)]
    one = (jnp.ones_like(m[0][0]), jnp.zeros_like(m[0][0]))
    a0 = dd_div(m[0], d[0])
    b = dd_sub(one, a0)
    rz1 = dd_mul(a0, dd_add(dd_mul(b, m[1]), dd_mul(a0, m[2])))
    p0 = dd_add(b, dd_div(rz1, m[0]))
    pq1 = dd_mul(a0, dd_add(dd_mul(p0, d[1]), dd_mul(a0, d[2])))
    a1 = dd_div(rz1, pq1)
    z0 = dd_sub(b, dd_mul(a1, p0))
    z1 = dd_sub(a0, dd_mul(a1, dd_sub(a0, p0)))
    z2 = dd_mul(a1, a0)
    rz2 = dd_mul(z2, dd_add(dd_add(dd_mul(z0, m[2]), dd_mul(z1, m[3])), dd_mul(z2, m[4])))
    be = dd_div(rz2, rz1)
    q0 = dd_add(z0, dd_mul(be, p0))
    q1 = dd_add(z1, dd_mul(be, a0))
    pq2 = dd_mul(z2, dd_add(dd_add(dd_mul(q0, d[2]), dd_mul(q1, d[3])), dd_mul(z2, d[4])))
    a2 = dd_div(rz2, pq2)
    xs = [
        dd_add(dd_add(a0, dd_mul(a1, p0)), dd_mul(a2, q0)),
        dd_add(dd_mul(a1, a0), dd_mul(a2, q1)),
        dd_mul(a2, z2),
    ]
    rs = [
        dd_sub(z0, dd_mul(a2, q0)),
        dd_sub(z1, dd_mul(a2, dd_sub(q1, q0))),
        dd_sub(z2, dd_mul(a2, dd_sub(z2, q1))),
        dd_mul(a2, z2),
    ]
    return [x[0] for x in xs], [r[0] for r in rs]


def faces(block):
    lane = iota((8, CZ), 1)
    group = ((lane + 4) // 8) % 16
    out = jnp.zeros((8, CZ), F32)
    for k in range(16):
        x, half = k // 2, k % 2
        tile = block[x, 8 * half : 8 * half + 8, :]
        out = jnp.where(group == k, pltpu.roll(tile, 8 * k, 1) if k else tile, out)
    return out


def spread_faces(plus, minus, out):
    lane = iota((8, CZ), 1)
    low = lane % 8 < 4
    upper = iota((8, CZ), 0) < 4
    keep = (lane < 4) | (lane >= 124)
    packs = {}
    for dx in (-1, 0, 1):
        for dy in (-1, 0, 1):
            i = (dx + 1) * 3 + dy + 1
            packs[dx, dy] = jnp.where(low, plus[i], minus[i])

    def moved(tile, k):
        return pltpu.roll(tile, CZ - 8 * k, 1) if k else tile

    for xp in range(EX):
        dx, x = (0, xp) if xp < 8 else ((1, xp - 8) if xp < 12 else (-1, xp - 8))
        for half in range(2):
            out[xp, 8 * half : 8 * half + 8, :] = jnp.where(keep, moved(packs[dx, 0], 2 * x + half), 0.0)
        both = jnp.where(upper, moved(packs[dx, 1], 2 * x), moved(packs[dx, -1], 2 * x + 1))
        out[xp, 16:24, :] = jnp.where(keep, both, 0.0)


def smooth_zy(m, a):
    lane = iota(m.shape, 1)
    first, last = lane == 0, lane == CZ - 1
    rm, ra = pltpu.roll(m, 1, 1), pltpu.roll(a, 1, 1)
    lm, la = pltpu.roll(m, CZ - 1, 1), pltpu.roll(a, CZ - 1, 1)
    m = m + 0.5 * (jnp.where(first, ra, rm) + jnp.where(last, la, lm))
    a = a + 0.5 * (jnp.where(first, rm, ra) + jnp.where(last, lm, la))

    def along_y(v):
        return v + 0.5 * (pltpu.roll(v, 1, 0) + pltpu.roll(v, EY - 1, 0))

    return along_y(m), along_y(a)


def kernel(
    owner_ref, dest_ref, prior_ref, h_ref, heat_ref,
    temp_out, resid_out, dep_out,
    heat, prior, hown, hm, ha, xm, ha_plus, ha_minus, xa, xa_plus, xa_minus,
    hy_plus, hy_minus, xy_plus, xy_minus, hpack, xpack, em, ea,
    send, held, rows, dsend, dheld, dtable, part_a, part_b, t_buf, r_buf,
    in_sem, out_sem, s1, r1, s2, r2, ds1, dr1, ds2, dr2, hs, hr, xs_, xr, as_, ar, bs, br,
):
    gx, gy, gz = lax.axis_index("gx"), lax.axis_index("gy"), lax.axis_index("gz")

    def at(a, b, c):
        return (lax.rem(gx + a + NX, NX), lax.rem(gy + b + NY, NY), lax.rem(gz + c + NZ, NZ))

    def remote(src, dst, ss, rs, to):
        return pltpu.make_async_remote_copy(
            src_ref=src, dst_ref=dst, send_sem=ss, recv_sem=rs, device_id=to, device_id_type=MESH
        )

    loads = [
        pltpu.make_async_copy(heat_ref, heat, in_sem.at[0]),
        pltpu.make_async_copy(h_ref, hown, in_sem.at[1]),
        pltpu.make_async_copy(prior_ref, prior, in_sem.at[2]),
    ]
    for c in loads:
        c.start()

    partners = set(AROUND)
    partners |= {(k, 0, 0) for k in range(1, NX)}
    partners |= {(0, j, l) for j in range(NY) for l in range(NZ)} - {(0, 0, 0)}
    partners = sorted({(a % NX, b % NY, c % NZ) for a, b, c in partners})
    barrier = pltpu.get_barrier_semaphore()
    for p in partners:
        pl.semaphore_signal(barrier, inc=1, device_id=at(*p), device_id_type=MESH)

    owner = owner_ref[...]
    dest = dest_ref[...]
    ox, oy = owner // NY, owner % NY
    kx = (ox - gx + NX) % NX
    jy = (oy - gy + NY) % NY
    rel = kx * NY + jy
    n_rows = owner.shape[1]
    named = rel == iota((NX * NY, n_rows), 0)
    earlier = (iota((n_rows, n_rows), 0) < iota((n_rows, n_rows), 1)).astype(F32).astype(BF16)
    rank = dot_nn(named.astype(F32).astype(BF16), earlier)
    rank_row = jnp.sum(jnp.where(named, rank, 0.0), axis=0, keepdims=True)
    slot = jy * CAP + rank_row.astype(jnp.int32)
    ahead = jnp.where(kx == iota((NX, n_rows), 0), (dest + 1).astype(F32), 0.0).astype(BF16)
    at_slot = (slot == iota((128, n_rows), 0)).astype(F32).astype(BF16)
    table = dot_nt(ahead, at_slot)
    dsend[...] = table.reshape(NX, 1, 128)
    dheld[0] = dsend[0]
    loads[0].wait()
    parts = three(heat[...])
    for c in range(CAP):
        mine = (named & (rank == float(c))).astype(F32).astype(BF16)
        packed = picked(mine, parts).reshape(NX, NY, CZ)
        send[:, :, c, :] = packed
        held[0, :, c, :] = packed[0]

    pl.semaphore_wait(barrier, len(partners))

    for k in range(1, NX):
        remote(dsend.at[k], dheld.at[k], ds1, dr1, at(k, 0, 0)).start()
    for k in range(1, NX):
        remote(send.at[k], held.at[k], s1, r1, at(k, 0, 0)).start()

    def exchange(own, wide, plus, minus, y_plus, y_minus, pack, ss, rs):
        for a, b in ((-1, 0), (1, 0), (0, -1), (0, 1), (-1, -1), (1, -1), (-1, 1), (1, 1)):
            xs = {-1: (0, 4), 0: (0, 8), 1: (4, 4)}[a]
            to = {-1: 8, 0: 0, 1: 12}[a]
            to_x = pl.ds(to, xs[1])
            from_x = pl.ds(*xs)
            if b == 0:
                remote(own.at[from_x], wide.at[to_x, pl.ds(0, CY)], ss.at[0], rs.at[0], at(a, b, 0)).start()
            elif b == -1:
                remote(own.at[from_x, pl.ds(0, 8)], y_plus.at[to_x], ss.at[1], rs.at[1], at(a, b, 0)).start()
            else:
                remote(own.at[from_x, pl.ds(8, 8)], y_minus.at[to_x], ss.at[2], rs.at[2], at(a, b, 0)).start()
        pack[...] = faces(own)
        for a in (-1, 0, 1):
            for b in (-1, 0, 1):
                i = (1 - a) * 3 + 1 - b
                remote(pack, plus.at[i], ss.at[3], rs.at[3], at(a, b, -1)).start()
                remote(pack, minus.at[i], ss.at[4], rs.at[4], at(a, b, 1)).start()

    def exchanged(wide, plus, minus, y_plus, y_minus, ss, rs):
        x_part = wide.at[pl.ds(8, 8), pl.ds(0, CY)]
        return [
            remote(v, v, ss.at[i], rs.at[i], at(1, 0, 0))
            for i, v in enumerate((x_part, y_plus, y_minus, plus, minus))
        ]

    loads[1].wait()
    exchange(hown, hm, ha_plus, ha_minus, hy_plus, hy_minus, hpack, hs, hr)
    hm[0:CX, 0:CY, :] = hown[...]

    d_along = remote(dsend.at[pl.ds(1, NX - 1)], dheld.at[pl.ds(1, NX - 1)], ds1, dr1, at(1, 0, 0))
    d_along.wait_recv()
    for j in range(1, NY):
        remote(dheld, dtable.at[j], ds2, dr2, at(0, j, 0)).start()

    h_waits = exchanged(hm, ha_plus, ha_minus, hy_plus, hy_minus, hs, hr)
    for w in h_waits:
        w.wait_recv()
    spread_faces(ha_plus, ha_minus, ha)
    upper = iota((EX, 8, CZ), 1) < 4
    hm[:, CY:EY, :] = jnp.where(upper, hy_plus[...], hy_minus[...])

    def inside(i, n):
        return (i < n - 1).astype(F32), (i > 0).astype(F32)

    (x_hi, x_lo), (y_hi, y_lo), (z_hi, z_lo) = inside(gx, NX), inside(gy, NY), inside(gz, NZ)
    row = iota((EY, CZ), 0)
    y_mask = jnp.where(row < CY, 1.0, jnp.where(row < CY + 4, y_hi, y_lo))
    z_mask = jnp.where(iota((EY, CZ), 1) < CZ // 2, z_hi, z_lo)
    for xp in range(EX):
        scale = y_mask if xp < CX else y_mask * (x_hi if xp < 12 else x_lo)
        h0 = hm[xp] * scale
        h1 = ha[xp] * (scale * z_mask)
        hm[xp] = h0
        ha[xp] = h1
        em[xp] = h0 * h0 / (1.0 + 10.5 * h0)
        ea[xp] = h1 * h1 / (1.0 + 10.5 * h1)

    along = remote(send.at[pl.ds(1, NX - 1)], held.at[pl.ds(1, NX - 1)], s1, r1, at(1, 0, 0))
    along.wait_recv()
    for j in range(1, NY):
        remote(held.at[:, j], rows.at[j], s2, r2, at(0, j, 0)).start()

    d_across = remote(dtable.at[pl.ds(1, NY - 1)], dtable.at[pl.ds(1, NY - 1)], ds2, dr2, at(0, 1, 0))
    d_across.wait_recv()
    dtable[0] = dheld[...]
    places = dtable[...].reshape(NY * NX, 128)
    own_lanes = iota((NY * NX, 128), 1) // CAP == iota((NY * NX, 128), 0) // NX
    places = jnp.where(own_lanes, places, 0.0).astype(BF16)
    cell = (iota((CX * CY, 128), 0) + 1).astype(F32)
    landing = []
    for c in range(CAP):
        lanes = (iota((CX * CY, 128), 1) % CAP == c).astype(F32).astype(BF16)
        landing.append((dot_nt(lanes, places) == cell).astype(F32).astype(BF16))
    landing = jnp.concatenate(landing, axis=1)

    across = remote(rows.at[pl.ds(1, NY - 1)], rows.at[pl.ds(1, NY - 1)], s2, r2, at(0, 1, 0))
    across.wait_recv()
    rows[0] = held[:, 0]
    arrived = jnp.concatenate([rows[:, :, c, :].reshape(NY * NX, CZ) for c in range(CAP)], axis=0)
    loads[2].wait()
    prior[...] = prior[...] + picked(landing, three(arrived)).reshape(CX, CY, CZ)
    dep_copy = pltpu.make_async_copy(prior, dep_out, out_sem.at[0])

    exchange(prior, xm, xa_plus, xa_minus, xy_plus, xy_minus, xpack, xs_, xr)
    dep_copy.start()
    xm[0:CX, 0:CY, :] = prior[...]
    x_waits = exchanged(xm, xa_plus, xa_minus, xy_plus, xy_minus, xs_, xr)
    for w in x_waits:
        w.wait_recv()
    spread_faces(xa_plus, xa_minus, xa)
    xm[:, CY:EY, :] = jnp.where(upper, xy_plus[...], xy_minus[...])

    def cells(width):
        return list(range(CX + width)) + list(range(EX - width, EX))

    def filtered(m, a, width):
        t = {x: smooth_zy(m[x], a[x]) for x in cells(width + 1)}
        out = {}
        for x in cells(width):
            lo, mid, hi = t[(x - 1) % EX], t[x], t[(x + 1) % EX]
            out[x] = tuple(mid[i] + 0.5 * (lo[i] + hi[i]) for i in range(2))
        return out

    m = {x: xm[x] * hm[x] for x in range(EX)}
    a = {x: xa[x] * ha[x] for x in range(EX)}
    us, gs = [], []
    for step in range(4):
        width = 3 - step
        t = filtered(m, a, width)
        um, ua = {}, {}
        for x in cells(width):
            um[x] = t[x][0] - m[x]
            ua[x] = t[x][1] - a[x]
            if step == 0:
                um[x] = um[x] - 10.5 * xm[x]
                ua[x] = ua[x] - 10.5 * xa[x]
        m = {x: em[x] * um[x] for x in cells(width)}
        a = {x: ea[x] * ua[x] for x in cells(width)}
        us.append([um[x][0:CY] for x in range(CX)])
        gs.append([m[x][0:CY] for x in range(CX)])

    us = [[halves(u) + (u,) for u in v] for v in us]
    gs_s = [[halves(g) + (g,) for g in v] for v in gs[:3]]
    row8 = iota((8, CZ), 0)
    lane8 = iota((8, CZ), 1)

    def pair_add(p, q):
        s, e = two_sum(p[0], q[0])
        return s, e + (p[1] + q[1])

    total = None
    for k, (i, j) in enumerate(((0, 0), (0, 1), (1, 1), (1, 2), (2, 2), (2, 3))):
        terms = []
        for x in range(CX):
            p, e = two_prod(gs_s[i][x][2], us[j][x][2], gs_s[i][x][:2], us[j][x][:2])
            terms += [(p[0:8], e[0:8]), (p[8:16], e[8:16])]
        v = tree(terms, pair_add)
        for shift in (4, 2, 1):
            v = pair_add(v, tuple(pltpu.roll(w, 8 - shift, 0) for w in v))
        v = pair_add(v, tuple(pltpu.roll(w, 64, 1) for w in v))
        v = jnp.where(lane8 < 64, v[0], v[1])
        total = v if total is None else jnp.where(row8 == k, v, total)
    part_a[0] = total

    def all_of(buf, n):
        s, e = tree([(buf[i], jnp.zeros((8, CZ), F32)) for i in range(n)], pair_add)
        return s + pltpu.roll(jnp.where(lane8 < 64, e, 0.0), 64, 1)

    for j in range(NY):
        for l in range(NZ):
            if j or l:
                remote(part_a.at[0], part_a.at[j * NZ + l], as_, ar, at(0, j, l)).start()
    a_all = remote(part_a.at[pl.ds(1, NY * NZ - 1)], part_a.at[pl.ds(1, NY * NZ - 1)], as_, ar, at(0, 1, 0))
    a_all.wait_recv()
    part_b[0] = all_of(part_a, NY * NZ)
    for k in range(1, NX):
        remote(part_b.at[0], part_b.at[k], bs, br, at(k, 0, 0)).start()
    b_all = remote(part_b.at[pl.ds(1, NX - 1)], part_b.at[pl.ds(1, NX - 1)], bs, br, at(1, 0, 0))
    b_all.wait_recv()
    s = all_of(part_b, NX)
    v = (s, pltpu.roll(s, 64, 1))
    for shift in (32, 16, 8, 4, 2, 1):
        v = pair_add(v, tuple(pltpu.roll(w, CZ - shift, 1) for w in v))
    v = quick_sum(*v)
    moments = [(v[0][k : k + 1, 0:1], v[1][k : k + 1, 0:1]) for k in range(6)]

    xs, rs = coefficients(moments)
    xs = [jnp.broadcast_to(c, (CY, CZ)) for c in xs]
    rs = [jnp.broadcast_to(c, (CY, CZ)) for c in rs]
    for x in range(CX):
        h = hown[x]
        over = 1.0 / h
        t_buf[x] = prior[x] + (xs[0] * gs[0][x] + xs[1] * gs[1][x] + xs[2] * gs[2][x]) * over
        mix = (rs[0] * gs[0][x] + rs[1] * gs[1][x]) + (rs[2] * gs[2][x] + rs[3] * gs[3][x])
        r_buf[x] = mix * (over + 10.5)
    outs = [
        pltpu.make_async_copy(t_buf, temp_out, out_sem.at[1]),
        pltpu.make_async_copy(r_buf, resid_out, out_sem.at[2]),
    ]
    for c in outs:
        c.start()
    for w in [d_along, along, d_across, across] + h_waits + x_waits + [a_all, b_all]:
        if w is d_across:
            for j in range(1, NY):
                remote(dheld, dtable.at[j], ds2, dr2, at(0, j, 0)).wait_send()
        else:
            w.wait_send()
    dep_copy.wait()
    for c in outs:
        c.wait()


def local(prior, h, heat, owner, dest):
    n = dest.shape[0]
    any_ = pl.BlockSpec(memory_space=pl.ANY)
    vmem = pl.BlockSpec(memory_space=pltpu.VMEM)
    block = jax.ShapeDtypeStruct((CX, CY, CZ), F32)
    V = lambda *shape: pltpu.VMEM(shape, F32)
    D = pltpu.SemaphoreType.DMA
    wide = V(EX, EY, CZ)
    nine, ys, tile = V(9, 8, CZ), V(EX, 8, CZ), V(8, CZ)
    own = V(CX, CY, CZ)
    scratch = [
        V(n, CZ), own, own, wide, wide, wide, nine, nine, wide, nine, nine,
        ys, ys, ys, ys, tile, tile, wide, wide,
        V(NX, NY, CAP, CZ), V(NX, NY, CAP, CZ), V(NY, NX, CAP, CZ),
        V(NX, 1, 128), V(NX, 1, 128), V(NY, NX, 1, 128),
        V(NY * NZ, 8, CZ), V(NX, 8, CZ), own, own,
        D((3,)), D((3,)), D, D, D, D, D, D, D, D,
        D((5,)), D((5,)), D((5,)), D((5,)), D, D, D, D,
    ]
    return pl.pallas_call(
        kernel,
        out_shape=(block, block, block),
        in_specs=[vmem, vmem, any_, any_, any_],
        out_specs=(any_, any_, any_),
        scratch_shapes=scratch,
        compiler_params=pltpu.CompilerParams(
            collective_id=0, has_side_effects=True, vmem_limit_bytes=48 * 1024 * 1024
        ),
    )(owner.reshape(1, n), dest.reshape(1, n), prior, h, heat)


def solution(mesh):
    placed = (
        P("gx", "gy", "gz"),
        P("gx", "gy", "gz"),
        P(("gx", "gy"), "gz"),
        P(("gx", "gy"), None),
        P(("gx", "gy")),
    )
    return jax.shard_map(
        local,
        mesh=mesh,
        in_specs=placed,
        out_specs=(P("gx", "gy", "gz"), P("gx", "gy", "gz"), P("gx", "gy", "gz")),
        check_vma=False,
    )
```

time: 689 us -> 66.5 us (0.10)
  blocking collectives: 502 us -> 0 us
  starting transfers between devices: 86.5 us -> 0 us
  waiting for transfers between devices: 75.5 us -> 0 us
  Pallas kernels: 0 us -> 60.4 us
  other arithmetic: 9.74 us -> 0 us
  between operations: 7.9 us -> 0.66 us
    psum x5 -> x0, blocking collectives: 502 us -> none  [the longest x3 298 us: rz_sum(): return lax.psum(jnp.sum(resid * precond), ('gx', 'gy', 'gz'))]
    pallas_call x0 -> x1, Pallas kernels: none -> 60.4 us  [local(): pl.pallas_call(kernel, out_shape=(block, block, block), in_specs=[vmem, v...]
    ppermute x24 -> x0, starting transfers between devices: 60.2 us -> none  [the longest x12 42.2 us: extended(): lax.ppermute(tail, axis, [(i, (i + 1) % count) for i in range(ends)])]
    ppermute x24 -> x0, waiting for transfers between devices: 42.6 us -> none  [the longest x12 40.5 us: extended(): lax.ppermute(head, axis, [((i + 1) % count, i) for i in range(ends)])]
    all_to_all x2 -> x0, waiting for transfers between devices: 32.9 us -> none  [the longest x1 20.3 us: local(): lax.all_to_all(send_heat.reshape(owners, capacity, local_third_span), ('g...]
    all_to_all x2 -> x0, starting transfers between devices: 26.2 us -> none  [the longest x1 20.6 us: local(): lax.all_to_all(send_slot.reshape(owners, capacity), ('gx', 'gy'), split_a...]
  transfers between devices with their start and end apart: 26 -> 0, of which waited for: 18 -> 0; matrix products, arithmetic and copies ran while one was open for 0% -> 0% of each run, Pallas kernels for 0% -> 0%
where the time goes in v1:
time: 66.5 us; the launch traced here: 66.3 us
  Pallas kernels  60.4 us (91%)
  local copies, waits for them, and re-layouts  5.15 us (8%)
    pallas_call x1, Pallas kernels, local(): pl.pallas_call(kernel, out_shape=(block, block, block), in_specs=[vmem, v...  60.4 us
    unnamed x13, local copies, waits for them, and re-layouts  5.15 us

profile of v1, /device:TPU:1, one launch (start us, length us, event | category | flops | bytes accessed | tf_op | source)
XLA Modules:
  0.0 66.3 jit_solution(9739878841837464252)
XLA Ops:
  0.6 0.0 copy-start.4
  0.6 0.0 copy-start.3
  0.7 0.7 copy-done.4
  1.3 0.0 copy-done.3
  1.3 0.0 copy-start
  1.3 0.9 %copy-done = f32[256,128]{1,0:T(8,128)S(1)} copy-done((f32[256,128]{1,0:T(8,128)S(1)}, f32[256,128]{1,0:T(8,128)}, u32[]{:S(2)}) %copy-start) | copy-done | bytes 131096
  2.2 0.0 copy-start.1
  2.2 0.8 %copy-done.1 = f32[8,16,128]{2,1,0:T(8,128)S(1)} copy-done((f32[8,16,128]{2,1,0:T(8,128)S(1)}, f32[8,16,128]{2,1,0:T(8,128)}, u32[]{:S(2)}) %copy-start.1) | copy-done | bytes 65560
  3.1 0.0 copy-start.2
  3.1 0.8 %copy-done.2 = f32[8,16,128]{2,1,0:T(8,128)S(1)} copy-done((f32[8,16,128]{2,1,0:T(8,128)S(1)}, f32[8,16,128]{2,1,0:T(8,128)}, u32[]{:S(2)}) %copy-start.2) | copy-done | bytes 65560
  3.9 60.4 %shard_map.76 = (f32[8,16,128]{2,1,0:T(8,128)S(1)}, f32[8,16,128]{2,1,0:T(8,128)S(1)}, f32[8,16,128]{2,1,0:T(8,128)S(1)}) custom-call(s32[1,256]{1,0:T(1,128)S(1)} %bitcast.2, s32[1,256]{1,0:T(1,128)S(1)} %bitcast.3, f32[8,16,128]{2,1,0:T(8,128)S(1)} %copy-done.1, f32[8,16,128]{2,1,0:T(8,128)S(1)} %copy-done.2, f32[256,128]{1,0:T(8,128)S(1)} %copy-done), custom_call_target="tpu_custom_call" | custom-call | tf_op jit(solution)/shard_map/pallas_call | solution.py:459
  64.4 0.6 copy.11
  65.0 0.6 copy.12
  65.6 0.6 copy.13
Async XLA Ops:
  0.6 0.7 %copy-start.4 = (s32[256]{0:T(256)S(1)}, s32[256]{0:T(256)}, u32[]{:S(2)}) copy-start(s32[256]{0:T(256)} %param.9) | copy-start | bytes 3076
  0.6 0.7 %copy-start.3 = (s32[256,1]{0,1:T(1,128)S(1)}, s32[256,1]{0,1:T(1,128)}, u32[]{:S(2)}) copy-start(s32[256,1]{0,1:T(1,128)} %param.8) | copy-start | bytes 3076
  1.3 0.9 %copy-start = (f32[256,128]{1,0:T(8,128)S(1)}, f32[256,128]{1,0:T(8,128)}, u32[]{:S(2)}) copy-start(f32[256,128]{1,0:T(8,128)} %heat_ref.1) | copy-start | bytes 393220
  2.2 0.8 %copy-start.1 = (f32[8,16,128]{2,1,0:T(8,128)S(1)}, f32[8,16,128]{2,1,0:T(8,128)}, u32[]{:S(2)}) copy-start(f32[8,16,128]{2,1,0:T(8,128)} %prior_ref.1) | copy-start | bytes 196612
  3.1 0.8 %copy-start.2 = (f32[8,16,128]{2,1,0:T(8,128)S(1)}, f32[8,16,128]{2,1,0:T(8,128)}, u32[]{:S(2)}) copy-start(f32[8,16,128]{2,1,0:T(8,128)} %h_ref.1) | copy-start | bytes 196612

commit v2 on v1

--- a/solution.py
+++ b/solution.py
@@ -1,5 +1,3 @@
-import functools
-
 import jax
 import jax.numpy as jnp
 from jax import lax
@@ -14,6 +12,9 @@
 CX, CY, CZ = 8, 16, 128
 EX, EY = 16, 24
 CAP = 4
+VMEM_BYTES = 60 * 1024 * 1024
+NEAR = 9
+FAR_FIRST = [8, 7, 9, 6, 10, 5, 11, 4, 12, 3, 13, 2, 14, 1, 15]
 AROUND = [(a, b, c) for a in (-1, 0, 1) for b in (-1, 0, 1) for c in (-1, 0, 1) if (a, b, c) != (0, 0, 0)]
 
 
@@ -181,7 +182,7 @@
 def kernel(
     owner_ref, dest_ref, prior_ref, h_ref, heat_ref,
     temp_out, resid_out, dep_out,
-    heat, prior, hown, hm, ha, xm, ha_plus, ha_minus, xa, xa_plus, xa_minus,
+    prior, owner_v, dest_v, heat, hown, hm, ha, xm, ha_plus, ha_minus, xa, xa_plus, xa_minus,
     hy_plus, hy_minus, xy_plus, xy_minus, hpack, xpack, em, ea,
     send, held, rows, dsend, dheld, dtable, part_a, part_b, t_buf, r_buf,
     in_sem, out_sem, s1, r1, s2, r2, ds1, dr1, ds2, dr2, hs, hr, xs_, xr, as_, ar, bs, br,
@@ -200,22 +201,24 @@
         pltpu.make_async_copy(heat_ref, heat, in_sem.at[0]),
         pltpu.make_async_copy(h_ref, hown, in_sem.at[1]),
         pltpu.make_async_copy(prior_ref, prior, in_sem.at[2]),
+        pltpu.make_async_copy(owner_ref, owner_v, in_sem.at[3]),
+        pltpu.make_async_copy(dest_ref, dest_v, in_sem.at[4]),
     ]
-    for c in loads:
+    for c in (loads[3], loads[4], loads[0], loads[1], loads[2]):
         c.start()
 
-    partners = set(AROUND)
-    partners |= {(k, 0, 0) for k in range(1, NX)}
-    partners |= {(0, j, l) for j in range(NY) for l in range(NZ)} - {(0, 0, 0)}
-    partners = sorted({(a % NX, b % NY, c % NZ) for a, b, c in partners})
+    partners = [(k, 0, 0) for k in FAR_FIRST] + [(0, j, 0) for j in (4, 3, 5, 2, 6, 1, 7)] + [(0, 0, l) for l in (2, 1, 3)]
     barrier = pltpu.get_barrier_semaphore()
     for p in partners:
         pl.semaphore_signal(barrier, inc=1, device_id=at(*p), device_id_type=MESH)
 
-    owner = owner_ref[...]
-    dest = dest_ref[...]
+    loads[3].wait()
+    loads[4].wait()
+    owner = owner_v[...]
+    dest = dest_v[...]
     ox, oy = owner // NY, owner % NY
     kx = (ox - gx + NX) % NX
+    kx = jnp.where(kx == 0, 0, jnp.where(kx <= NX // 2, 2 * kx - 1, 2 * NX - 2 * kx))
     jy = (oy - gy + NY) % NY
     rel = kx * NY + jy
     n_rows = owner.shape[1]
@@ -239,10 +242,14 @@
 
     pl.semaphore_wait(barrier, len(partners))
 
-    for k in range(1, NX):
-        remote(dsend.at[k], dheld.at[k], ds1, dr1, at(k, 0, 0)).start()
-    for k in range(1, NX):
-        remote(send.at[k], held.at[k], s1, r1, at(k, 0, 0)).start()
+    def place(k):
+        return 2 * k - 1 if k <= NX // 2 else 2 * NX - 2 * k
+
+    for k in FAR_FIRST:
+        remote(dsend.at[place(k)], dheld.at[place(k)], ds1, dr1, at(k, 0, 0)).start()
+    for k in FAR_FIRST:
+        i = int(place(k) >= NEAR)
+        remote(send.at[place(k)], held.at[place(k)], s1.at[i], r1.at[i], at(k, 0, 0)).start()
 
     def exchange(own, wide, plus, minus, y_plus, y_minus, pack, ss, rs):
         for a, b in ((-1, 0), (1, 0), (0, -1), (0, 1), (-1, -1), (1, -1), (-1, 1), (1, 1)):
@@ -270,14 +277,53 @@
             for i, v in enumerate((x_part, y_plus, y_minus, plus, minus))
         ]
 
-    loads[1].wait()
-    exchange(hown, hm, ha_plus, ha_minus, hy_plus, hy_minus, hpack, hs, hr)
-    hm[0:CX, 0:CY, :] = hown[...]
-
     d_along = remote(dsend.at[pl.ds(1, NX - 1)], dheld.at[pl.ds(1, NX - 1)], ds1, dr1, at(1, 0, 0))
     d_along.wait_recv()
     for j in range(1, NY):
         remote(dheld, dtable.at[j], ds2, dr2, at(0, j, 0)).start()
+
+    chunks = ((1, NEAR), (NEAR, NX))
+    along = []
+    for i, (lo, hi) in enumerate(chunks):
+        part = pl.ds(lo, hi - lo)
+        along.append(remote(send.at[part], held.at[part], s1.at[i], r1.at[i], at(1, 0, 0)))
+        along[i].wait_recv()
+        part = pl.ds(lo if i else 0, hi - (lo if i else 0))
+        for j in range(1, NY):
+            remote(held.at[part, j], rows.at[j, part], s2.at[i], r2.at[i], at(0, j, 0)).start()
+
+    d_across = remote(dtable.at[pl.ds(1, NY - 1)], dtable.at[pl.ds(1, NY - 1)], ds2, dr2, at(0, 1, 0))
+    d_across.wait_recv()
+    dtable[0] = dheld[...]
+
+    loads[1].wait()
+    exchange(hown, hm, ha_plus, ha_minus, hy_plus, hy_minus, hpack, hs, hr)
+    hm[0:CX, 0:CY, :] = hown[...]
+
+    places = dtable[...].reshape(NY * NX, 128)
+    own_lanes = iota((NY * NX, 128), 1) // CAP == iota((NY * NX, 128), 0) // NX
+    places = jnp.where(own_lanes, places, 0.0).astype(BF16)
+    cell = (iota((CX * CY, 128), 0) + 1).astype(F32)
+    landing = []
+    for c in range(CAP):
+        lanes = (iota((CX * CY, 128), 1) % CAP == c).astype(F32).astype(BF16)
+        landing.append((dot_nt(lanes, places) == cell).astype(F32).astype(BF16))
+    landing = jnp.concatenate(landing, axis=1)
+
+    across = []
+    for i, (lo, hi) in enumerate(chunks):
+        part = pl.ds(lo if i else 0, hi - (lo if i else 0))
+        across.append(remote(rows.at[pl.ds(1, NY - 1), part], rows.at[pl.ds(1, NY - 1), part], s2.at[i], r2.at[i], at(0, 1, 0)))
+        across[i].wait_recv()
+    rows[0] = held[:, 0]
+    arrived = jnp.concatenate([rows[:, :, c, :].reshape(NY * NX, CZ) for c in range(CAP)], axis=0)
+    loads[2].wait()
+    prior[...] = prior[...] + picked(landing, three(arrived)).reshape(CX, CY, CZ)
+
+    exchange(prior, xm, xa_plus, xa_minus, xy_plus, xy_minus, xpack, xs_, xr)
+    dep_copy = pltpu.make_async_copy(prior, dep_out, out_sem.at[0])
+    dep_copy.start()
+    xm[0:CX, 0:CY, :] = prior[...]
 
     h_waits = exchanged(hm, ha_plus, ha_minus, hy_plus, hy_minus, hs, hr)
     for w in h_waits:
@@ -302,35 +348,6 @@
         em[xp] = h0 * h0 / (1.0 + 10.5 * h0)
         ea[xp] = h1 * h1 / (1.0 + 10.5 * h1)
 
-    along = remote(send.at[pl.ds(1, NX - 1)], held.at[pl.ds(1, NX - 1)], s1, r1, at(1, 0, 0))
-    along.wait_recv()
-    for j in range(1, NY):
-        remote(held.at[:, j], rows.at[j], s2, r2, at(0, j, 0)).start()
-
-    d_across = remote(dtable.at[pl.ds(1, NY - 1)], dtable.at[pl.ds(1, NY - 1)], ds2, dr2, at(0, 1, 0))
-    d_across.wait_recv()
-    dtable[0] = dheld[...]
-    places = dtable[...].reshape(NY * NX, 128)
-    own_lanes = iota((NY * NX, 128), 1) // CAP == iota((NY * NX, 128), 0) // NX
-    places = jnp.where(own_lanes, places, 0.0).astype(BF16)
-    cell = (iota((CX * CY, 128), 0) + 1).astype(F32)
-    landing = []
-    for c in range(CAP):
-        lanes = (iota((CX * CY, 128), 1) % CAP == c).astype(F32).astype(BF16)
-        landing.append((dot_nt(lanes, places) == cell).astype(F32).astype(BF16))
-    landing = jnp.concatenate(landing, axis=1)
-
-    across = remote(rows.at[pl.ds(1, NY - 1)], rows.at[pl.ds(1, NY - 1)], s2, r2, at(0, 1, 0))
-    across.wait_recv()
-    rows[0] = held[:, 0]
-    arrived = jnp.concatenate([rows[:, :, c, :].reshape(NY * NX, CZ) for c in range(CAP)], axis=0)
-    loads[2].wait()
-    prior[...] = prior[...] + picked(landing, three(arrived)).reshape(CX, CY, CZ)
-    dep_copy = pltpu.make_async_copy(prior, dep_out, out_sem.at[0])
-
-    exchange(prior, xm, xa_plus, xa_minus, xy_plus, xy_minus, xpack, xs_, xr)
-    dep_copy.start()
-    xm[0:CX, 0:CY, :] = prior[...]
     x_waits = exchanged(xm, xa_plus, xa_minus, xy_plus, xy_minus, xs_, xr)
     for w in x_waits:
         w.wait_recv()
@@ -375,7 +392,7 @@
         s, e = two_sum(p[0], q[0])
         return s, e + (p[1] + q[1])
 
-    total = None
+    high, rest = jnp.zeros((8, CZ), F32), jnp.zeros((8, CZ), F32)
     for k, (i, j) in enumerate(((0, 0), (0, 1), (1, 1), (1, 2), (2, 2), (2, 3))):
         terms = []
         for x in range(CX):
@@ -383,33 +400,35 @@
             terms += [(p[0:8], e[0:8]), (p[8:16], e[8:16])]
         v = tree(terms, pair_add)
         for shift in (4, 2, 1):
-            v = pair_add(v, tuple(pltpu.roll(w, 8 - shift, 0) for w in v))
-        v = pair_add(v, tuple(pltpu.roll(w, 64, 1) for w in v))
-        v = jnp.where(lane8 < 64, v[0], v[1])
-        total = v if total is None else jnp.where(row8 == k, v, total)
-    part_a[0] = total
+            v = pair_add(v, tuple(pltpu.roll(w, shift, 0) for w in v))
+        high, rest = jnp.where(row8 == k, v[0], high), jnp.where(row8 == k, v[1], rest)
+    v = high, rest
+    for shift in (64, 32, 16, 8, 4, 2, 1):
+        v = pair_add(v, tuple(pltpu.roll(w, shift, 1) for w in v))
+    v = jnp.where(lane8 == row8, v[0], jnp.where(lane8 == row8 + 64, v[1], 0.0))
+    part_a[0] = jnp.sum(v, axis=0, keepdims=True)
 
     def all_of(buf, n):
-        s, e = tree([(buf[i], jnp.zeros((8, CZ), F32)) for i in range(n)], pair_add)
-        return s + pltpu.roll(jnp.where(lane8 < 64, e, 0.0), 64, 1)
-
-    for j in range(NY):
-        for l in range(NZ):
+        v = buf[...].reshape(n, CZ)
+        v = tree([(v[8 * i : 8 * i + 8], jnp.zeros((8, CZ), F32)) for i in range(n // 8)], pair_add)
+        for shift in (4, 2, 1):
+            v = pair_add(v, tuple(pltpu.roll(w, shift, 0) for w in v))
+        v = v[0] + pltpu.roll(jnp.where(lane8 < 64, v[1], 0.0), 64, 1)
+        return v[0:1]
+
+    for l in (2, 1, 3, 0):
+        for j in (4, 3, 5, 2, 6, 1, 7, 0):
             if j or l:
                 remote(part_a.at[0], part_a.at[j * NZ + l], as_, ar, at(0, j, l)).start()
     a_all = remote(part_a.at[pl.ds(1, NY * NZ - 1)], part_a.at[pl.ds(1, NY * NZ - 1)], as_, ar, at(0, 1, 0))
     a_all.wait_recv()
     part_b[0] = all_of(part_a, NY * NZ)
-    for k in range(1, NX):
+    for k in FAR_FIRST:
         remote(part_b.at[0], part_b.at[k], bs, br, at(k, 0, 0)).start()
     b_all = remote(part_b.at[pl.ds(1, NX - 1)], part_b.at[pl.ds(1, NX - 1)], bs, br, at(1, 0, 0))
     b_all.wait_recv()
     s = all_of(part_b, NX)
-    v = (s, pltpu.roll(s, 64, 1))
-    for shift in (32, 16, 8, 4, 2, 1):
-        v = pair_add(v, tuple(pltpu.roll(w, CZ - shift, 1) for w in v))
-    v = quick_sum(*v)
-    moments = [(v[0][k : k + 1, 0:1], v[1][k : k + 1, 0:1]) for k in range(6)]
+    moments = [quick_sum(s[:, k : k + 1], s[:, 64 + k : 65 + k]) for k in range(6)]
 
     xs, rs = coefficients(moments)
     xs = [jnp.broadcast_to(c, (CY, CZ)) for c in xs]
@@ -426,21 +445,28 @@
     ]
     for c in outs:
         c.start()
-    for w in [d_along, along, d_across, across] + h_waits + x_waits + [a_all, b_all]:
-        if w is d_across:
-            for j in range(1, NY):
-                remote(dheld, dtable.at[j], ds2, dr2, at(0, j, 0)).wait_send()
-        else:
-            w.wait_send()
+    for w in [d_along] + along + across + h_waits + x_waits + [a_all, b_all]:
+        w.wait_send()
+    for j in range(1, NY):
+        remote(dheld, dtable.at[j], ds2, dr2, at(0, j, 0)).wait_send()
     dep_copy.wait()
     for c in outs:
         c.wait()
 
 
+def write_out(*refs):
+    sems = refs[-1]
+    n = len(refs) // 2
+    copies = [pltpu.make_async_copy(refs[i], refs[n + i], sems.at[i]) for i in range(n)]
+    for c in copies:
+        c.start()
+    for c in copies:
+        c.wait()
+
+
 def local(prior, h, heat, owner, dest):
     n = dest.shape[0]
-    any_ = pl.BlockSpec(memory_space=pl.ANY)
-    vmem = pl.BlockSpec(memory_space=pltpu.VMEM)
+    hbm = pl.BlockSpec(memory_space=pltpu.HBM)
     block = jax.ShapeDtypeStruct((CX, CY, CZ), F32)
     V = lambda *shape: pltpu.VMEM(shape, F32)
     D = pltpu.SemaphoreType.DMA
@@ -448,24 +474,32 @@
     nine, ys, tile = V(9, 8, CZ), V(EX, 8, CZ), V(8, CZ)
     own = V(CX, CY, CZ)
     scratch = [
-        V(n, CZ), own, own, wide, wide, wide, nine, nine, wide, nine, nine,
+        own, pltpu.VMEM((1, n), jnp.int32), pltpu.VMEM((1, n), jnp.int32), V(n, CZ), own, wide, wide, wide, nine, nine, wide, nine, nine,
         ys, ys, ys, ys, tile, tile, wide, wide,
         V(NX, NY, CAP, CZ), V(NX, NY, CAP, CZ), V(NY, NX, CAP, CZ),
         V(NX, 1, 128), V(NX, 1, 128), V(NY, NX, 1, 128),
-        V(NY * NZ, 8, CZ), V(NX, 8, CZ), own, own,
-        D((3,)), D((3,)), D, D, D, D, D, D, D, D,
+        V(NY * NZ, 1, CZ), V(NX, 1, CZ), own, own,
+        D((5,)), D((3,)), D((2,)), D((2,)), D((2,)), D((2,)), D, D, D, D,
         D((5,)), D((5,)), D((5,)), D((5,)), D, D, D, D,
     ]
-    return pl.pallas_call(
+    outs = pl.pallas_call(
         kernel,
         out_shape=(block, block, block),
-        in_specs=[vmem, vmem, any_, any_, any_],
-        out_specs=(any_, any_, any_),
+        in_specs=[hbm] * 5,
+        out_specs=(hbm,) * 3,
         scratch_shapes=scratch,
         compiler_params=pltpu.CompilerParams(
-            collective_id=0, has_side_effects=True, vmem_limit_bytes=48 * 1024 * 1024
+            collective_id=0, has_side_effects=True, vmem_limit_bytes=VMEM_BYTES
         ),
     )(owner.reshape(1, n), dest.reshape(1, n), prior, h, heat)
+    return pl.pallas_call(
+        write_out,
+        out_shape=(block, block, block),
+        in_specs=[hbm] * 3,
+        out_specs=(hbm,) * 3,
+        scratch_shapes=[D((3,))],
+        compiler_params=pltpu.CompilerParams(vmem_limit_bytes=VMEM_BYTES),
+    )(*outs)
 
 
 def solution(mesh):

time: 66.5 us -> 63.9 us (0.961)
  local copies, waits for them, and re-layouts: 5.15 us -> 0 us
  Pallas kernels: 60.4 us -> 63.1 us
    unnamed x13 -> x0, local copies, waits for them, and re-layouts: 5.15 us -> none
    pallas_call x1 -> x2, Pallas kernels: 60.4 us -> 63.1 us  [the longest x1 56 us: local(): pl.pallas_call(kernel, out_shape=(block, block, block), in_specs=[hbm] *...]
where the time goes in v2:
time: 63.9 us; the launch traced here: 63.7 us
  Pallas kernels  63.1 us (99%)
  between operations  0.64 us (1%)
    pallas_call x1, Pallas kernels, local(): pl.pallas_call(kernel, out_shape=(block, block, block), in_specs=[hbm] *...  56 us
    pallas_call x1, Pallas kernels, local(): pl.pallas_call(write_out, out_shape=(block, block, block), in_specs=[hbm]...  7.09 us

profile of v2, /device:TPU:1, one launch (start us, length us, event | category | flops | bytes accessed | tf_op | source)
XLA Modules:
  0.0 63.7 jit_solution(15868910629838502409)
XLA Ops:
  0.6 56.0 %shard_map.76 = (f32[8,16,128]{2,1,0:T(8,128)}, f32[8,16,128]{2,1,0:T(8,128)}, f32[8,16,128]{2,1,0:T(8,128)}) custom-call(s32[1,256]{1,0:T(1,128)} %bitcast.2, s32[1,256]{1,0:T(1,128)} %bitcast.3, f32[8,16,128]{2,1,0:T(8,128)} %prior_ref.1, f32[8,16,128]{2,1,0:T(8,128)} %h_ref.1, f32[256,128]{1,0:T(8,128)} %heat_ref.1), custom_call_target="tpu_custom_call" | custom-call | tf_op jit(solution)/shard_map/pallas_call | solution.py:485
  56.7 7.1 %shard_map.77 = (f32[8,16,128]{2,1,0:T(8,128)}, f32[8,16,128]{2,1,0:T(8,128)}, f32[8,16,128]{2,1,0:T(8,128)}) custom-call(f32[8,16,128]{2,1,0:T(8,128)} %get-tuple-element.6.refs_0_, f32[8,16,128]{2,1,0:T(8,128)} %get-tuple-element.7.refs_1_, f32[8,16,128]{2,1,0:T(8,128)} %get-tuple-element.8.refs_2_), custom_call_target="tpu_custom_call" | custom-call | tf_op jit(solution)/shard_map/pallas_call | solution.py:495

commit v3 on v2

--- a/solution.py
+++ b/solution.py
@@ -13,7 +13,6 @@
 EX, EY = 16, 24
 CAP = 4
 VMEM_BYTES = 60 * 1024 * 1024
-NEAR = 9
 FAR_FIRST = [8, 7, 9, 6, 10, 5, 11, 4, 12, 3, 13, 2, 14, 1, 15]
 AROUND = [(a, b, c) for a in (-1, 0, 1) for b in (-1, 0, 1) for c in (-1, 0, 1) if (a, b, c) != (0, 0, 0)]
 
@@ -181,11 +180,11 @@
 
 def kernel(
     owner_ref, dest_ref, prior_ref, h_ref, heat_ref,
-    temp_out, resid_out, dep_out,
-    prior, owner_v, dest_v, heat, hown, hm, ha, xm, ha_plus, ha_minus, xa, xa_plus, xa_minus,
+    temp_out, resid_out, added_out,
+    added, prior, owner_v, dest_v, heat, hown, hm, ha, xm, ha_plus, ha_minus, xa, xa_plus, xa_minus,
     hy_plus, hy_minus, xy_plus, xy_minus, hpack, xpack, em, ea,
-    send, held, rows, dsend, dheld, dtable, part_a, part_b, t_buf, r_buf,
-    in_sem, out_sem, s1, r1, s2, r2, ds1, dr1, ds2, dr2, hs, hr, xs_, xr, as_, ar, bs, br,
+    send, rows, dsend, dheld, dtable, part_a, part_b, t_buf, r_buf,
+    in_sem, out_sem, s1, r1, ds1, dr1, ds2, dr2, hs, hr, xs_, xr, as_, ar, bs, br,
 ):
     gx, gy, gz = lax.axis_index("gx"), lax.axis_index("gy"), lax.axis_index("gz")
 
@@ -207,7 +206,8 @@
     for c in (loads[3], loads[4], loads[0], loads[1], loads[2]):
         c.start()
 
-    partners = [(k, 0, 0) for k in FAR_FIRST] + [(0, j, 0) for j in (4, 3, 5, 2, 6, 1, 7)] + [(0, 0, l) for l in (2, 1, 3)]
+    others = [(k, j, 0) for k in FAR_FIRST + [0] for j in (4, 3, 5, 2, 6, 1, 7, 0) if k or j]
+    partners = others + [(0, 0, l) for l in (2, 1, 3)]
     barrier = pltpu.get_barrier_semaphore()
     for p in partners:
         pl.semaphore_signal(barrier, inc=1, device_id=at(*p), device_id_type=MESH)
@@ -238,7 +238,7 @@
         mine = (named & (rank == float(c))).astype(F32).astype(BF16)
         packed = picked(mine, parts).reshape(NX, NY, CZ)
         send[:, :, c, :] = packed
-        held[0, :, c, :] = packed[0]
+        rows[0, 0, c, :] = packed[0, 0]
 
     pl.semaphore_wait(barrier, len(partners))
 
@@ -247,9 +247,9 @@
 
     for k in FAR_FIRST:
         remote(dsend.at[place(k)], dheld.at[place(k)], ds1, dr1, at(k, 0, 0)).start()
-    for k in FAR_FIRST:
-        i = int(place(k) >= NEAR)
-        remote(send.at[place(k)], held.at[place(k)], s1.at[i], r1.at[i], at(k, 0, 0)).start()
+    for k, j, _ in others:
+        q, i = place(k) if k else 0, int(j > 0)
+        remote(send.at[q, j], rows.at[j, q], s1.at[i], r1.at[i], at(k, j, 0)).start()
 
     def exchange(own, wide, plus, minus, y_plus, y_minus, pack, ss, rs):
         for a, b in ((-1, 0), (1, 0), (0, -1), (0, 1), (-1, -1), (1, -1), (-1, 1), (1, 1)):
@@ -282,16 +282,6 @@
     for j in range(1, NY):
         remote(dheld, dtable.at[j], ds2, dr2, at(0, j, 0)).start()
 
-    chunks = ((1, NEAR), (NEAR, NX))
-    along = []
-    for i, (lo, hi) in enumerate(chunks):
-        part = pl.ds(lo, hi - lo)
-        along.append(remote(send.at[part], held.at[part], s1.at[i], r1.at[i], at(1, 0, 0)))
-        along[i].wait_recv()
-        part = pl.ds(lo if i else 0, hi - (lo if i else 0))
-        for j in range(1, NY):
-            remote(held.at[part, j], rows.at[j, part], s2.at[i], r2.at[i], at(0, j, 0)).start()
-
     d_across = remote(dtable.at[pl.ds(1, NY - 1)], dtable.at[pl.ds(1, NY - 1)], ds2, dr2, at(0, 1, 0))
     d_across.wait_recv()
     dtable[0] = dheld[...]
@@ -310,19 +300,20 @@
         landing.append((dot_nt(lanes, places) == cell).astype(F32).astype(BF16))
     landing = jnp.concatenate(landing, axis=1)
 
-    across = []
-    for i, (lo, hi) in enumerate(chunks):
-        part = pl.ds(lo if i else 0, hi - (lo if i else 0))
-        across.append(remote(rows.at[pl.ds(1, NY - 1), part], rows.at[pl.ds(1, NY - 1), part], s2.at[i], r2.at[i], at(0, 1, 0)))
-        across[i].wait_recv()
-    rows[0] = held[:, 0]
+    came = [
+        remote(rows.at[0, pl.ds(1, NX - 1)], rows.at[0, pl.ds(1, NX - 1)], s1.at[0], r1.at[0], at(1, 0, 0)),
+        remote(rows.at[pl.ds(1, NY - 1)], rows.at[pl.ds(1, NY - 1)], s1.at[1], r1.at[1], at(0, 1, 0)),
+    ]
+    for w in came:
+        w.wait_recv()
     arrived = jnp.concatenate([rows[:, :, c, :].reshape(NY * NX, CZ) for c in range(CAP)], axis=0)
+    added[...] = picked(landing, three(arrived)).reshape(CX, CY, CZ)
     loads[2].wait()
-    prior[...] = prior[...] + picked(landing, three(arrived)).reshape(CX, CY, CZ)
+    prior[...] = prior[...] + added[...]
 
     exchange(prior, xm, xa_plus, xa_minus, xy_plus, xy_minus, xpack, xs_, xr)
-    dep_copy = pltpu.make_async_copy(prior, dep_out, out_sem.at[0])
-    dep_copy.start()
+    added_copy = pltpu.make_async_copy(added, added_out, out_sem.at[0])
+    added_copy.start()
     xm[0:CX, 0:CY, :] = prior[...]
 
     h_waits = exchanged(hm, ha_plus, ha_minus, hy_plus, hy_minus, hs, hr)
@@ -434,33 +425,20 @@
     xs = [jnp.broadcast_to(c, (CY, CZ)) for c in xs]
     rs = [jnp.broadcast_to(c, (CY, CZ)) for c in rs]
     for x in range(CX):
-        h = hown[x]
-        over = 1.0 / h
-        t_buf[x] = prior[x] + (xs[0] * gs[0][x] + xs[1] * gs[1][x] + xs[2] * gs[2][x]) * over
-        mix = (rs[0] * gs[0][x] + rs[1] * gs[1][x]) + (rs[2] * gs[2][x] + rs[3] * gs[3][x])
-        r_buf[x] = mix * (over + 10.5)
+        t_buf[x] = xs[0] * gs[0][x] + xs[1] * gs[1][x] + xs[2] * gs[2][x]
+        r_buf[x] = (rs[0] * gs[0][x] + rs[1] * gs[1][x]) + (rs[2] * gs[2][x] + rs[3] * gs[3][x])
     outs = [
         pltpu.make_async_copy(t_buf, temp_out, out_sem.at[1]),
         pltpu.make_async_copy(r_buf, resid_out, out_sem.at[2]),
     ]
     for c in outs:
         c.start()
-    for w in [d_along] + along + across + h_waits + x_waits + [a_all, b_all]:
+    for w in [d_along] + came + h_waits + x_waits + [a_all, b_all]:
         w.wait_send()
     for j in range(1, NY):
         remote(dheld, dtable.at[j], ds2, dr2, at(0, j, 0)).wait_send()
-    dep_copy.wait()
+    added_copy.wait()
     for c in outs:
-        c.wait()
-
-
-def write_out(*refs):
-    sems = refs[-1]
-    n = len(refs) // 2
-    copies = [pltpu.make_async_copy(refs[i], refs[n + i], sems.at[i]) for i in range(n)]
-    for c in copies:
-        c.start()
-    for c in copies:
         c.wait()
 
 
@@ -474,15 +452,15 @@
     nine, ys, tile = V(9, 8, CZ), V(EX, 8, CZ), V(8, CZ)
     own = V(CX, CY, CZ)
     scratch = [
-        own, pltpu.VMEM((1, n), jnp.int32), pltpu.VMEM((1, n), jnp.int32), V(n, CZ), own, wide, wide, wide, nine, nine, wide, nine, nine,
+        own, own, pltpu.VMEM((1, n), jnp.int32), pltpu.VMEM((1, n), jnp.int32), V(n, CZ), own, wide, wide, wide, nine, nine, wide, nine, nine,
         ys, ys, ys, ys, tile, tile, wide, wide,
-        V(NX, NY, CAP, CZ), V(NX, NY, CAP, CZ), V(NY, NX, CAP, CZ),
+        V(NX, NY, CAP, CZ), V(NY, NX, CAP, CZ),
         V(NX, 1, 128), V(NX, 1, 128), V(NY, NX, 1, 128),
         V(NY * NZ, 1, CZ), V(NX, 1, CZ), own, own,
-        D((5,)), D((3,)), D((2,)), D((2,)), D((2,)), D((2,)), D, D, D, D,
+        D((5,)), D((3,)), D((2,)), D((2,)), D, D, D, D,
         D((5,)), D((5,)), D((5,)), D((5,)), D, D, D, D,
     ]
-    outs = pl.pallas_call(
+    step, rest, added = pl.pallas_call(
         kernel,
         out_shape=(block, block, block),
         in_specs=[hbm] * 5,
@@ -492,14 +470,9 @@
             collective_id=0, has_side_effects=True, vmem_limit_bytes=VMEM_BYTES
         ),
     )(owner.reshape(1, n), dest.reshape(1, n), prior, h, heat)
-    return pl.pallas_call(
-        write_out,
-        out_shape=(block, block, block),
-        in_specs=[hbm] * 3,
-        out_specs=(hbm,) * 3,
-        scratch_shapes=[D((3,))],
-        compiler_params=pltpu.CompilerParams(vmem_limit_bytes=VMEM_BYTES),
-    )(*outs)
+    deposited = prior + added
+    over = 1.0 / h
+    return deposited + step * over, rest * (over + 10.5), deposited
 
 
 def solution(mesh):

time: 63.9 us -> 56.3 us (0.88)
  Pallas kernels: 63.1 us -> 53.8 us
  other arithmetic: 0 us -> 1.59 us
    pallas_call x1 -> x0, Pallas kernels: 7.09 us -> none  [local(): pl.pallas_call(write_out, out_shape=(block, block, block), in_specs=[hbm]...]
    pallas_call x1, Pallas kernels: 56 us -> 53.8 us  [local(): pl.pallas_call(kernel, out_shape=(block, block, block), in_specs=[hbm] *...]
    add x0 -> x1, other arithmetic: none -> 1.59 us  [local(): return (deposited + step * over, rest * (over + 10.5), deposited)]
where the time goes in v3:
time: 56.3 us; the launch traced here: 56.1 us
  Pallas kernels  53.8 us (96%)
  other arithmetic  1.59 us (3%)
  between operations  0.67 us (1%)
    pallas_call x1, Pallas kernels, local(): pl.pallas_call(kernel, out_shape=(block, block, block), in_specs=[hbm] *...  53.8 us
    add x1, other arithmetic, local(): return (deposited + step * over, rest * (over + 10.5), deposited)  1.59 us

profile of v3, /device:TPU:1, one launch (start us, length us, event | category | flops | bytes accessed | tf_op | source)
XLA Modules:
  0.0 56.1 jit_solution(12110029899457606637)
XLA Ops:
  0.6 0.0 copy-start
  0.6 0.0 copy-start.1
  0.7 53.8 %shard_map.76 = (f32[8,16,128]{2,1,0:T(8,128)}, f32[8,16,128]{2,1,0:T(8,128)}, f32[8,16,128]{2,1,0:T(8,128)}) custom-call(s32[1,256]{1,0:T(1,128)} %bitcast.2, s32[1,256]{1,0:T(1,128)} %bitcast.3, f32[8,16,128]{2,1,0:T(8,128)} %prior_ref.1, f32[8,16,128]{2,1,0:T(8,128)} %h_ref.1, f32[256,128]{1,0:T(8,128)} %heat_ref.1), custom_call_target="tpu_custom_call" | custom-call | tf_op jit(solution)/shard_map/pallas_call | solution.py:463
  54.5 0.0 copy-done
  54.5 0.0 copy-done.1
  54.5 1.6 %multiply_add_fusion = (f32[8,16,128]{2,1,0:T(8,128)}, f32[8,16,128]{2,1,0:T(8,128)}, f32[8,16,128]{2,1,0:T(8,128)}) fusion(f32[8,16,128]{2,1,0:T(8,128)} %get-tuple-element.7, f32[8,16,128]{2,1,0:T(8,128)S(1)} %copy-done.1, f32[8,16,128]{2,1,0:T(8,128)S(1)} %copy-done, f32[8,16,128]{2,1,0:T(8,128)} %get-tuple-element.6, f32[8,16,128]{2,1,0:T(8,128)} %get-tuple-element.8), kind=kLoop, calls=%fused_computation.1 | loop fusion | flops 98304 | bytes 524288 | tf_op jit(solution)/shard_map/add | solution.py:475
Async XLA Ops:
  0.6 53.8 %copy-start = (f32[8,16,128]{2,1,0:T(8,128)S(1)}, f32[8,16,128]{2,1,0:T(8,128)}, u32[]{:S(2)}) copy-start(f32[8,16,128]{2,1,0:T(8,128)} %prior_ref.1) | copy-start | bytes 196612
  0.6 53.8 %copy-start.1 = (f32[8,16,128]{2,1,0:T(8,128)S(1)}, f32[8,16,128]{2,1,0:T(8,128)}, u32[]{:S(2)}) copy-start(f32[8,16,128]{2,1,0:T(8,128)} %h_ref.1) | copy-start | bytes 196612

commit v4 on v3

--- a/solution.py
+++ b/solution.py
@@ -12,8 +12,10 @@
 CX, CY, CZ = 8, 16, 128
 EX, EY = 16, 24
 CAP = 4
-VMEM_BYTES = 60 * 1024 * 1024
-FAR_FIRST = [8, 7, 9, 6, 10, 5, 11, 4, 12, 3, 13, 2, 14, 1, 15]
+VMEM_BYTES = 54992 * 1024
+FAR = [8, 7, 9, 6, 10, 5, 11]
+CLOSE = [4, 12, 3, 13, 2, 14, 1, 15]
+REACH = 4
 AROUND = [(a, b, c) for a in (-1, 0, 1) for b in (-1, 0, 1) for c in (-1, 0, 1) if (a, b, c) != (0, 0, 0)]
 
 
@@ -89,8 +91,7 @@
     q = a[0] / b[0]
     r = dd_sub(a, dd_mul((q, jnp.zeros_like(q)), b))
     q2 = r[0] / b[0]
-    r = dd_sub(r, dd_mul((q2, jnp.zeros_like(q)), b))
-    return dd_add(quick_sum(q, q2), (r[0] / b[0], jnp.zeros_like(q)))
+    return quick_sum(q, q2)
 
 
 def tree(values, add):
@@ -180,11 +181,11 @@
 
 def kernel(
     owner_ref, dest_ref, prior_ref, h_ref, heat_ref,
-    temp_out, resid_out, added_out,
-    added, prior, owner_v, dest_v, heat, hown, hm, ha, xm, ha_plus, ha_minus, xa, xa_plus, xa_minus,
+    t_buf, r_buf, added,
+    prior, owner_v, dest_v, heat, hown, hm, ha, xm, ha_plus, ha_minus, xa, xa_plus, xa_minus,
     hy_plus, hy_minus, xy_plus, xy_minus, hpack, xpack, em, ea,
-    send, rows, dsend, dheld, dtable, part_a, part_b, t_buf, r_buf,
-    in_sem, out_sem, s1, r1, ds1, dr1, ds2, dr2, hs, hr, xs_, xr, as_, ar, bs, br,
+    send, rows, dsend, dheld, dtable, part_a, part_b,
+    in_sem, s1, r1, ds1, dr1, ds2, dr2, hs, hr, xs_, xr, as_, ar, bs, br,
 ):
     gx, gy, gz = lax.axis_index("gx"), lax.axis_index("gy"), lax.axis_index("gz")
 
@@ -206,8 +207,11 @@
     for c in (loads[3], loads[4], loads[0], loads[1], loads[2]):
         c.start()
 
-    others = [(k, j, 0) for k in FAR_FIRST + [0] for j in (4, 3, 5, 2, 6, 1, 7, 0) if k or j]
-    partners = others + [(0, 0, l) for l in (2, 1, 3)]
+    def group(ks):
+        return [(k, j, 0) for k in ks for j in (4, 3, 5, 2, 6, 1, 7, 0) if k or j]
+
+    others = group(FAR + CLOSE + [0])
+    partners = others + [(0, 0, 2)] + [(0, 0, 1), (0, 0, 3)]
     barrier = pltpu.get_barrier_semaphore()
     for p in partners:
         pl.semaphore_signal(barrier, inc=1, device_id=at(*p), device_id_type=MESH)
@@ -240,17 +244,10 @@
         send[:, :, c, :] = packed
         rows[0, 0, c, :] = packed[0, 0]
 
+    loads[1].wait()
+    hpack[...] = faces(hown)
+
     pl.semaphore_wait(barrier, len(partners))
-
-    def place(k):
-        return 2 * k - 1 if k <= NX // 2 else 2 * NX - 2 * k
-
-    for k in FAR_FIRST:
-        remote(dsend.at[place(k)], dheld.at[place(k)], ds1, dr1, at(k, 0, 0)).start()
-    for k, j, _ in others:
-        q, i = place(k) if k else 0, int(j > 0)
-        remote(send.at[q, j], rows.at[j, q], s1.at[i], r1.at[i], at(k, j, 0)).start()
-
     def exchange(own, wide, plus, minus, y_plus, y_minus, pack, ss, rs):
         for a, b in ((-1, 0), (1, 0), (0, -1), (0, 1), (-1, -1), (1, -1), (-1, 1), (1, 1)):
             xs = {-1: (0, 4), 0: (0, 8), 1: (4, 4)}[a]
@@ -263,7 +260,6 @@
                 remote(own.at[from_x, pl.ds(0, 8)], y_plus.at[to_x], ss.at[1], rs.at[1], at(a, b, 0)).start()
             else:
                 remote(own.at[from_x, pl.ds(8, 8)], y_minus.at[to_x], ss.at[2], rs.at[2], at(a, b, 0)).start()
-        pack[...] = faces(own)
         for a in (-1, 0, 1):
             for b in (-1, 0, 1):
                 i = (1 - a) * 3 + 1 - b
@@ -277,6 +273,20 @@
             for i, v in enumerate((x_part, y_plus, y_minus, plus, minus))
         ]
 
+
+    def place(k):
+        return 2 * k - 1 if k <= NX // 2 else 2 * NX - 2 * k
+
+    def send_rows(ks):
+        for k in ks:
+            if k:
+                remote(dsend.at[place(k)], dheld.at[place(k)], ds1, dr1, at(k, 0, 0)).start()
+        for k, j, _ in group(ks):
+            q, i = place(k) if k else 0, int(j > 0)
+            remote(send.at[q, j], rows.at[j, q], s1.at[i], r1.at[i], at(k, j, 0)).start()
+
+    send_rows(FAR + CLOSE + [0])
+
     d_along = remote(dsend.at[pl.ds(1, NX - 1)], dheld.at[pl.ds(1, NX - 1)], ds1, dr1, at(1, 0, 0))
     d_along.wait_recv()
     for j in range(1, NY):
@@ -285,11 +295,8 @@
     d_across = remote(dtable.at[pl.ds(1, NY - 1)], dtable.at[pl.ds(1, NY - 1)], ds2, dr2, at(0, 1, 0))
     d_across.wait_recv()
     dtable[0] = dheld[...]
-
-    loads[1].wait()
     exchange(hown, hm, ha_plus, ha_minus, hy_plus, hy_minus, hpack, hs, hr)
     hm[0:CX, 0:CY, :] = hown[...]
-
     places = dtable[...].reshape(NY * NX, 128)
     own_lanes = iota((NY * NX, 128), 1) // CAP == iota((NY * NX, 128), 0) // NX
     places = jnp.where(own_lanes, places, 0.0).astype(BF16)
@@ -311,9 +318,8 @@
     loads[2].wait()
     prior[...] = prior[...] + added[...]
 
+    xpack[...] = faces(prior)
     exchange(prior, xm, xa_plus, xa_minus, xy_plus, xy_minus, xpack, xs_, xr)
-    added_copy = pltpu.make_async_copy(added, added_out, out_sem.at[0])
-    added_copy.start()
     xm[0:CX, 0:CY, :] = prior[...]
 
     h_waits = exchanged(hm, ha_plus, ha_minus, hy_plus, hy_minus, hs, hr)
@@ -414,7 +420,7 @@
     a_all = remote(part_a.at[pl.ds(1, NY * NZ - 1)], part_a.at[pl.ds(1, NY * NZ - 1)], as_, ar, at(0, 1, 0))
     a_all.wait_recv()
     part_b[0] = all_of(part_a, NY * NZ)
-    for k in FAR_FIRST:
+    for k in FAR + CLOSE:
         remote(part_b.at[0], part_b.at[k], bs, br, at(k, 0, 0)).start()
     b_all = remote(part_b.at[pl.ds(1, NX - 1)], part_b.at[pl.ds(1, NX - 1)], bs, br, at(1, 0, 0))
     b_all.wait_recv()
@@ -427,23 +433,15 @@
     for x in range(CX):
         t_buf[x] = xs[0] * gs[0][x] + xs[1] * gs[1][x] + xs[2] * gs[2][x]
         r_buf[x] = (rs[0] * gs[0][x] + rs[1] * gs[1][x]) + (rs[2] * gs[2][x] + rs[3] * gs[3][x])
-    outs = [
-        pltpu.make_async_copy(t_buf, temp_out, out_sem.at[1]),
-        pltpu.make_async_copy(r_buf, resid_out, out_sem.at[2]),
-    ]
-    for c in outs:
-        c.start()
     for w in [d_along] + came + h_waits + x_waits + [a_all, b_all]:
         w.wait_send()
     for j in range(1, NY):
         remote(dheld, dtable.at[j], ds2, dr2, at(0, j, 0)).wait_send()
-    added_copy.wait()
-    for c in outs:
-        c.wait()
 
 
 def local(prior, h, heat, owner, dest):
     n = dest.shape[0]
+    vmem = pl.BlockSpec(memory_space=pltpu.VMEM)
     hbm = pl.BlockSpec(memory_space=pltpu.HBM)
     block = jax.ShapeDtypeStruct((CX, CY, CZ), F32)
     V = lambda *shape: pltpu.VMEM(shape, F32)
@@ -452,19 +450,19 @@
     nine, ys, tile = V(9, 8, CZ), V(EX, 8, CZ), V(8, CZ)
     own = V(CX, CY, CZ)
     scratch = [
-        own, own, pltpu.VMEM((1, n), jnp.int32), pltpu.VMEM((1, n), jnp.int32), V(n, CZ), own, wide, wide, wide, nine, nine, wide, nine, nine,
+        own, pltpu.VMEM((1, n), jnp.int32), pltpu.VMEM((1, n), jnp.int32), V(n, CZ), own, wide, wide, wide, nine, nine, wide, nine, nine,
         ys, ys, ys, ys, tile, tile, wide, wide,
         V(NX, NY, CAP, CZ), V(NY, NX, CAP, CZ),
         V(NX, 1, 128), V(NX, 1, 128), V(NY, NX, 1, 128),
-        V(NY * NZ, 1, CZ), V(NX, 1, CZ), own, own,
-        D((5,)), D((3,)), D((2,)), D((2,)), D, D, D, D,
+        V(NY * NZ, 1, CZ), V(NX, 1, CZ),
+        D((5,)), D((2,)), D((2,)), D, D, D, D,
         D((5,)), D((5,)), D((5,)), D((5,)), D, D, D, D,
     ]
     step, rest, added = pl.pallas_call(
         kernel,
         out_shape=(block, block, block),
         in_specs=[hbm] * 5,
-        out_specs=(hbm,) * 3,
+        out_specs=(vmem,) * 3,
         scratch_shapes=scratch,
         compiler_params=pltpu.CompilerParams(
             collective_id=0, has_side_effects=True, vmem_limit_bytes=VMEM_BYTES

time: 56.3 us -> 55.3 us (0.982)
  other arithmetic: 1.59 us -> 0.69 us
  Pallas kernels: 53.8 us -> 53.1 us
  local copies, waits for them, and re-layouts: 0.01 us -> 0.69 us
    add x1, other arithmetic: 1.59 us -> 0.69 us  [local(): return (deposited + step * over, rest * (over + 10.5), deposited)]
    pallas_call x1, Pallas kernels: 53.8 us -> 53.1 us  [local(): pl.pallas_call(kernel, out_shape=(block, block, block), in_specs=[hbm] *...]
    unnamed x4 -> x8, local copies, waits for them, and re-layouts: 0.01 us -> 0.69 us
where the time goes in v4:
time: 55.3 us; the launch traced here: 55.2 us
  Pallas kernels  53.1 us (96%)
  local copies, waits for them, and re-layouts  0.69 us (1%)
  other arithmetic  0.69 us (1%)
  between operations  0.67 us (1%)
    pallas_call x1, Pallas kernels, local(): pl.pallas_call(kernel, out_shape=(block, block, block), in_specs=[hbm] *...  53.1 us

profile of v4, /device:TPU:1, one launch (start us, length us, event | category | flops | bytes accessed | tf_op | source)
XLA Modules:
  0.0 55.2 jit_solution(8923535191216490487)
XLA Ops:
  0.6 0.0 copy-start.1
  0.6 0.0 copy-start
  0.7 0.7 %copy-done.1 = s32[256]{0:T(256)S(1)} copy-done((s32[256]{0:T(256)S(1)}, s32[256]{0:T(256)}, u32[]{:S(2)}) %copy-start.1) | copy-done | bytes 1048
  1.3 0.0 copy-done
  1.3 0.0 copy-start.2
  1.3 0.0 copy-start.3
  1.3 53.1 %shard_map.76 = (f32[8,16,128]{2,1,0:T(8,128)S(1)}, f32[8,16,128]{2,1,0:T(8,128)S(1)}, f32[8,16,128]{2,1,0:T(8,128)S(1)}) custom-call(s32[1,256]{1,0:T(1,128)S(1)} %bitcast.2, s32[1,256]{1,0:T(1,128)S(1)} %bitcast.3, f32[8,16,128]{2,1,0:T(8,128)} %prior_ref.1, f32[8,16,128]{2,1,0:T(8,128)} %h_ref.1, f32[256,128]{1,0:T(8,128)} %heat_ref.1), custom_call_target="tpu_custom_call" | custom-call | tf_op jit(solution)/shard_map/pallas_call | solution.py:461
  54.5 0.0 copy-done.2
  54.5 0.0 copy-done.3
  54.5 0.7 %multiply_add_fusion = (f32[8,16,128]{2,1,0:T(8,128)}, f32[8,16,128]{2,1,0:T(8,128)}, f32[8,16,128]{2,1,0:T(8,128)}) fusion(f32[8,16,128]{2,1,0:T(8,128)S(1)} %get-tuple-element.7, f32[8,16,128]{2,1,0:T(8,128)S(1)} %copy-done.3, f32[8,16,128]{2,1,0:T(8,128)S(1)} %copy-done.2, f32[8,16,128]{2,1,0:T(8,128)S(1)} %get-tuple-element.6, ...), kind=kLoop, calls=%fused_computation.1 | loop fusion | flops 98304 | bytes 524288 | tf_op jit(solution)/shard_map/add | solution.py:473
Async XLA Ops:
  0.6 0.7 %copy-start.1 = (s32[256]{0:T(256)S(1)}, s32[256]{0:T(256)}, u32[]{:S(2)}) copy-start(s32[256]{0:T(256)} %param.9) | copy-start | bytes 3076
  0.6 0.7 %copy-start = (s32[256,1]{0,1:T(1,128)S(1)}, s32[256,1]{0,1:T(1,128)}, u32[]{:S(2)}) copy-start(s32[256,1]{0,1:T(1,128)} %param.8) | copy-start | bytes 3076
  1.3 53.1 %copy-start.2 = (f32[8,16,128]{2,1,0:T(8,128)S(1)}, f32[8,16,128]{2,1,0:T(8,128)}, u32[]{:S(2)}) copy-start(f32[8,16,128]{2,1,0:T(8,128)} %prior_ref.1) | copy-start | bytes 196612
  1.3 53.1 %copy-start.3 = (f32[8,16,128]{2,1,0:T(8,128)S(1)}, f32[8,16,128]{2,1,0:T(8,128)}, u32[]{:S(2)}) copy-start(f32[8,16,128]{2,1,0:T(8,128)} %h_ref.1) | copy-start | bytes 196612

commit v5 on v4

--- a/solution.py
+++ b/solution.py
@@ -248,8 +248,8 @@
     hpack[...] = faces(hown)
 
     pl.semaphore_wait(barrier, len(partners))
-    def exchange(own, wide, plus, minus, y_plus, y_minus, pack, ss, rs):
-        for a, b in ((-1, 0), (1, 0), (0, -1), (0, 1), (-1, -1), (1, -1), (-1, 1), (1, 1)):
+    def exchange(own, wide, plus, minus, y_plus, y_minus, pack, ss, rs, ready=None):
+        for a, b in ((-1, -1), (1, -1), (-1, 1), (1, 1), (-1, 0), (1, 0), (0, -1), (0, 1)):
             xs = {-1: (0, 4), 0: (0, 8), 1: (4, 4)}[a]
             to = {-1: 8, 0: 0, 1: 12}[a]
             to_x = pl.ds(to, xs[1])
@@ -260,8 +260,10 @@
                 remote(own.at[from_x, pl.ds(0, 8)], y_plus.at[to_x], ss.at[1], rs.at[1], at(a, b, 0)).start()
             else:
                 remote(own.at[from_x, pl.ds(8, 8)], y_minus.at[to_x], ss.at[2], rs.at[2], at(a, b, 0)).start()
-        for a in (-1, 0, 1):
-            for b in (-1, 0, 1):
+        if ready is None:
+            pack[...] = faces(own)
+        for a in (-1, 1, 0):
+            for b in (-1, 1, 0):
                 i = (1 - a) * 3 + 1 - b
                 remote(pack, plus.at[i], ss.at[3], rs.at[3], at(a, b, -1)).start()
                 remote(pack, minus.at[i], ss.at[4], rs.at[4], at(a, b, 1)).start()
@@ -295,7 +297,7 @@
     d_across = remote(dtable.at[pl.ds(1, NY - 1)], dtable.at[pl.ds(1, NY - 1)], ds2, dr2, at(0, 1, 0))
     d_across.wait_recv()
     dtable[0] = dheld[...]
-    exchange(hown, hm, ha_plus, ha_minus, hy_plus, hy_minus, hpack, hs, hr)
+    exchange(hown, hm, ha_plus, ha_minus, hy_plus, hy_minus, hpack, hs, hr, ready=True)
     hm[0:CX, 0:CY, :] = hown[...]
     places = dtable[...].reshape(NY * NX, 128)
     own_lanes = iota((NY * NX, 128), 1) // CAP == iota((NY * NX, 128), 0) // NX
@@ -318,7 +320,6 @@
     loads[2].wait()
     prior[...] = prior[...] + added[...]
 
-    xpack[...] = faces(prior)
     exchange(prior, xm, xa_plus, xa_minus, xy_plus, xy_minus, xpack, xs_, xr)
     xm[0:CX, 0:CY, :] = prior[...]
 

time: 55.3 us -> 55.3 us (level)
  no operation moved by 1% of the time
where the time goes in v5:
time: 55.3 us; the launch traced here: 55.2 us
  Pallas kernels  53.1 us (96%)
  local copies, waits for them, and re-layouts  0.69 us (1%)
  other arithmetic  0.69 us (1%)
  between operations  0.67 us (1%)
    pallas_call x1, Pallas kernels, local(): pl.pallas_call(kernel, out_shape=(block, block, block), in_specs=[hbm] *...  53.1 us

profile of v5, /device:TPU:1, one launch (start us, length us, event | category | flops | bytes accessed | tf_op | source)
XLA Modules:
  0.0 55.2 jit_solution(9636880337292102382)
XLA Ops:
  0.6 0.0 copy-start.1
  0.6 0.0 copy-start
  0.7 0.7 %copy-done.1 = s32[256]{0:T(256)S(1)} copy-done((s32[256]{0:T(256)S(1)}, s32[256]{0:T(256)}, u32[]{:S(2)}) %copy-start.1) | copy-done | bytes 1048
  1.3 0.0 copy-done
  1.3 0.0 copy-start.2
  1.3 0.0 copy-start.3
  1.3 53.1 %shard_map.76 = (f32[8,16,128]{2,1,0:T(8,128)S(1)}, f32[8,16,128]{2,1,0:T(8,128)S(1)}, f32[8,16,128]{2,1,0:T(8,128)S(1)}) custom-call(s32[1,256]{1,0:T(1,128)S(1)} %bitcast.2, s32[1,256]{1,0:T(1,128)S(1)} %bitcast.3, f32[8,16,128]{2,1,0:T(8,128)} %prior_ref.1, f32[8,16,128]{2,1,0:T(8,128)} %h_ref.1, f32[256,128]{1,0:T(8,128)} %heat_ref.1), custom_call_target="tpu_custom_call" | custom-call | tf_op jit(solution)/shard_map/pallas_call | solution.py:462
  54.5 0.0 copy-done.2
  54.5 0.0 copy-done.3
  54.5 0.7 %multiply_add_fusion = (f32[8,16,128]{2,1,0:T(8,128)}, f32[8,16,128]{2,1,0:T(8,128)}, f32[8,16,128]{2,1,0:T(8,128)}) fusion(f32[8,16,128]{2,1,0:T(8,128)S(1)} %get-tuple-element.7, f32[8,16,128]{2,1,0:T(8,128)S(1)} %copy-done.3, f32[8,16,128]{2,1,0:T(8,128)S(1)} %copy-done.2, f32[8,16,128]{2,1,0:T(8,128)S(1)} %get-tuple-element.6, ...), kind=kLoop, calls=%fused_computation.1 | loop fusion | flops 98304 | bytes 524288 | tf_op jit(solution)/shard_map/add | solution.py:474
Async XLA Ops:
  0.6 0.7 %copy-start.1 = (s32[256]{0:T(256)S(1)}, s32[256]{0:T(256)}, u32[]{:S(2)}) copy-start(s32[256]{0:T(256)} %param.9) | copy-start | bytes 3076
  0.6 0.7 %copy-start = (s32[256,1]{0,1:T(1,128)S(1)}, s32[256,1]{0,1:T(1,128)}, u32[]{:S(2)}) copy-start(s32[256,1]{0,1:T(1,128)} %param.8) | copy-start | bytes 3076
  1.3 53.2 %copy-start.2 = (f32[8,16,128]{2,1,0:T(8,128)S(1)}, f32[8,16,128]{2,1,0:T(8,128)}, u32[]{:S(2)}) copy-start(f32[8,16,128]{2,1,0:T(8,128)} %prior_ref.1) | copy-start | bytes 196612
  1.3 53.2 %copy-start.3 = (f32[8,16,128]{2,1,0:T(8,128)S(1)}, f32[8,16,128]{2,1,0:T(8,128)}, u32[]{:S(2)}) copy-start(f32[8,16,128]{2,1,0:T(8,128)} %h_ref.1) | copy-start | bytes 196612
